TPU v7x, 32 devices: a whole 2x2x4 slice. The times are simulated.
32 devices in a mesh: rad: 4 (over y, core), mode: 8 (over z, x).
Axes of the slice: x: 2, y: 2, z: 4, core: 2. Of those that a mesh axis runs over, the one named last changes fastest.
Arguments:
- spectra: bfloat16 [2, 128, 1024, 1024], P(None, 'mode', 'rad'), may hold values from -6 to 6
- diffusivity: float32 [1024], replicated, may hold values from 0.1 to 1
- eigenvalues: float32 [1024], replicated, may hold values from 0.3 to 3
- radial_basis: bfloat16 [1024, 1024], replicated, may hold values from -0.1875 to 0.1875
- dual_basis: bfloat16 [1024, 1024], replicated, may hold values from -0.1875 to 0.1875
- degree_count: int32 [128], replicated, may hold values from 1 to 1024, as said below
- order_slot: int32 [128], replicated, may hold values from 0 to 127, as said below
Outputs:
- stepped: bfloat16 [2, 128, 1024, 1024], P(None, 'mode', 'rad')
Inputs may be any that keep to these rules, and one draw needn't show every extreme that they name: `degree_count`: row i holds order m_i = floor(i * 4); at most 1024 - m_i of its slots are live, and row 0 has all 1024. `order_slot`: A permutation of the rows. Output row d * 16 + s * 2 + k takes an input row of block s, that is one of s * 16 to (s + 1) * 16 - 1.
All inputs are finite; a program needn't handle non-finite values.
Results may differ from a plain program's by a relative error of at most 0.0065.
Values may be sent and summed in bfloat16 or wider, within the bound.
A program may use at most 192 MiB of HBM per device.

v0:
```python
import jax
import jax.numpy as jnp
from jax import lax
from jax.sharding import PartitionSpec as P


def extended(shard, sides, width):
    for axis, dim in sides:
        count, length = (lax.axis_size(axis), shard.shape[dim])
        up = [(i, (i + 1) % count) for i in range(count - 1)]
        down = [(j, i) for i, j in up]
        last = lax.slice_in_dim(shard, length - width, length, axis=dim)
        first = lax.slice_in_dim(shard, 0, width, axis=dim)
        before = lax.ppermute(last, axis, up)
        after = lax.ppermute(first, axis, down)
        shard = jnp.concatenate([before, shard, after], axis=dim)
    return shard


def degree_table(
    counts, order_start, order_rows, slot_start, slot_width, slots_total, orders_total
):
    row_ids = order_start + jnp.arange(order_rows, dtype=jnp.int32)
    orders = row_ids * slots_total // (2 * orders_total)
    slot_ids = slot_start + jnp.arange(slot_width, dtype=jnp.int32)
    degree = (orders[:, None] + slot_ids[None, :]).astype(jnp.float32)
    limits = lax.dynamic_slice_in_dim(counts, order_start, order_rows)
    live_mask = slot_ids[None, :] < limits[:, None]
    return (degree, live_mask)


def explicit(padded, kappa_rows, radius_start, degree, live_mask, shells_total):
    center = padded[:, :, 2:-2]
    shell_rows = center.shape[2]
    second = (
        -padded[:, :, :-4]
        + 16.0 * padded[:, :, 1:-3]
        - 30.0 * center
        + 16.0 * padded[:, :, 3:-1]
        - padded[:, :, 4:]
    ) / 12.0
    radius = (
        1.2
        + (radius_start + jnp.arange(shell_rows, dtype=jnp.int32)).astype(jnp.float32)
        / shells_total
    )
    damping = (degree * (degree + 1.0))[None, :, None, :] / ((shells_total * radius) ** 2)[
        None, None, :, None
    ]
    updated = center + 0.5 * kappa_rows[None, None, :, None] * (second - damping * center)
    return jnp.where(live_mask[None, :, None, :], updated, 0.0).astype(jnp.bfloat16)


def on_device(
    spectra, diffusivity, eigenvalues, radial_basis, dual_basis, degree_count, order_slot
):
    orders_here = spectra.shape[1]
    shells_here = spectra.shape[2]
    slots_total = spectra.shape[3]
    shells_total = diffusivity.shape[0]
    orders_total = degree_count.shape[0]
    groups = lax.axis_size("mode")
    shell_groups = lax.axis_size("rad")
    per_group = orders_here // groups
    window = slots_total // shell_groups
    group_index = lax.axis_index("mode")
    order_start = group_index * orders_here
    slot_start = lax.axis_index("rad") * window
    degree_win, live_win = degree_table(
        degree_count, order_start, orders_here, slot_start, window, slots_total, orders_total
    )
    degree_all, live_all = degree_table(
        degree_count, order_start, orders_here, 0, slots_total, slots_total, orders_total
    )
    padded = extended(spectra, (("rad", 2),), 2).astype(jnp.float32)
    radius_start = lax.axis_index("rad") * shells_here
    kappa_rows = lax.dynamic_slice_in_dim(diffusivity, radius_start, shells_here)
    updated = explicit(padded, kappa_rows, radius_start, degree_all, live_all, shells_total)
    relaid = lax.all_to_all(updated, "rad", split_axis=3, concat_axis=2, tiled=True)
    identity = jnp.eye(shells_total, dtype=jnp.float32)
    basis_full = (identity + radial_basis.astype(jnp.float32)).astype(jnp.bfloat16)
    dual_full = (identity + dual_basis.astype(jnp.float32)).astype(jnp.bfloat16)
    projected = jnp.einsum("kr,cirj->cikj", dual_full, relaid, preferred_element_type=jnp.float32)
    divisor = eigenvalues[None, None, :, None] + 0.5 * (degree_win * (degree_win + 1.0))[
        None, :, None, :
    ] / (shells_total * shells_total)
    scaled = (projected / divisor).astype(jnp.bfloat16)
    restored = jnp.einsum("kr,cirj->cikj", basis_full, scaled, preferred_element_type=jnp.float32)
    solved = jnp.where(live_win[None, :, None, :], restored, 0.0).astype(jnp.bfloat16)
    targets = lax.dynamic_slice_in_dim(
        order_slot.reshape(groups, orders_here), group_index * per_group, per_group, 1
    )
    picked_rows = targets.reshape(orders_here) - order_start
    sendable = jnp.take(solved, picked_rows, axis=1)
    stepped = lax.all_to_all(
        lax.all_to_all(sendable, "rad", split_axis=2, concat_axis=3, tiled=True),
        "mode",
        split_axis=1,
        concat_axis=1,
        tiled=True,
    )
    return stepped


def solution(mesh):
    placed = (P(None, "mode", "rad", None), P(), P(), P(), P(), P(), P())
    return jax.shard_map(
        on_device,
        mesh=mesh,
        in_specs=placed,
        out_specs=P(None, "mode", "rad", None),
        check_vma=False,
    )
```

profile of v0, /device:TPU:25, one launch (start us, length us, event | category | flops | bytes accessed | tf_op | source)
XLA Modules:
  0.0 1069.9 jit_solution(16511757446988110815)
XLA Ops:
  0.0 1.4 fusion.20
  1.4 3.7 collective-permute-start
  5.1 1.9 collective-permute-start.1
  7.1 0.1 add_multiply_fusion
  7.2 0.7 dynamic_slice.11
  7.9 8.4 broadcast_divide_fusion
  16.3 0.1 iota_compare_fusion.1
  16.4 0.8 dynamic-slice_multiply_fusion
  17.1 0.0 collective-permute-done
  17.1 0.0 collective-permute-done.1
  17.1 19.2 %maximum_convert_fusion = f32[2,16,260,1024]{3,2,1,0:T(8,128)} fusion(bf16[2,16,2,1024]{3,2,1,0:T(2,128)(2,1)S(1)} %collective-permute-done.1, bf16[2,16,256,1024]{3,2,1,0:T(8,128)(2,1)} %param.7, bf16[2,16,2,1024]{3,2,1,0:T(2,128)(2,1)S(1)} %collective-permute-done), kind=kLoop, calls=%fused_computation.17 | loop fusion | flops 51118080 | bytes 51118080 | tf_op jit(solution)/shard_map/convert_element_type | solution.py:75
  36.3 65.6 %fusion.5 = bf16[2,16,256,1024]{3,2,1,0:T(8,128)(2,1)} fusion(f32[2,16,260,1024]{3,2,1,0:T(8,128)} %maximum_convert_fusion, f32[16,256,1024]{2,1,0:T(8,128)} %broadcast_divide_fusion, f32[256]{0:T(256)S(1)} %dynamic-slice_multiply_fusion, pred[16,1024]{1,0:T(8,128)(4,1)S(1)} %iota_compare_fusion.1), kind=kLoop, calls=%fused_computation.7 | loop fusion | flops 125829120 | bytes 201344000 | tf_op jit(solution)/shard_map/convert_element_type | solution.py:51
  101.9 23.7 %copy.16 = bf16[2,16,256,1024]{2,1,0,3:T(8,128)(2,1)} copy(bf16[2,16,256,1024]{3,2,1,0:T(8,128)(2,1)} %fusion.5) | data formatting | bytes 33554432 | tf_op jit(solution)/shard_map/convert_element_type | solution.py:51
  125.6 0.0 copy-start.1
  125.6 0.0 copy-start
  125.6 7.3 all-to-all-start
  133.0 0.0 copy-done.1
  133.0 0.1 reshape.176
  133.1 0.1 dynamic-slice_subtract_fusion
  133.1 0.1 sub.45
  133.2 0.1 sub.39
  133.3 0.1 broadcast_compare_fusion
  133.4 0.1 fusion.18
  133.5 0.0 copy-done
  133.5 6.9 broadcast_add_fusion
  140.4 171.9 %all-to-all-done = bf16[2,16,256,1024]{2,1,0,3:T(8,128)(2,1)} async-done(((bf16[2,16,256,1024]{2,1,0,3:T(8,128)(2,1)}), bf16[2,16,256,1024]{2,1,0,3:T(8,128)(2,1)}, u32[]{:S(2)}, u32[]{:S(2)}) %all-to-all-start) | async-done | bytes 16777248 | tf_op jit(solution)/shard_map/all_to_all | solution.py:79
  312.3 0.0 copy-start.2
  312.3 26.3 %copy.18 = bf16[2,16,4,256,256]{4,3,2,1,0:T(8,128)(2,1)} copy(bf16[2,16,4,256,256]{3,1,0,4,2:T(8,128)(2,1)} %bitcast.2) | data formatting | bytes 33554432 | tf_op jit(solution)/shard_map/all_to_all | solution.py:79
  338.6 0.0 copy-done.2
  338.6 27.6 %fusion.9.clone.7 = bf16[2,16,1024,256]{2,3,1,0:T(8,128)(2,1)} fusion(bf16[2,16,1024,256]{3,2,1,0:T(8,128)(2,1)} %bitcast.54, f32[16,1024,256]{1,2,0:T(8,128)} %broadcast_add_fusion, bf16[1024,1024]{1,0:T(8,128)(2,1)S(1)} %copy-done.2), kind=kOutput, calls=%fused_computation.15.clone.clone.clone.clone.clone.2 | convolution fusion | flops 17201889280 | bytes 52428800 | tf_op jit(solution)/shard_map/kr,cirj->cikj/dot_general | solution.py:83
  366.3 27.5 %fusion.10 = bf16[2,16,1024,256]{2,3,1,0:T(8,128)(2,1)} fusion(pred[16,256]{1,0:T(8,128)(4,1)S(1)} %broadcast_compare_fusion, bf16[1024,1024]{1,0:T(8,128)(2,1)} %param.10, bf16[2,16,1024,256]{2,3,1,0:T(8,128)(2,1)} %fusion.9.clone.7), kind=kOutput, calls=%fused_computation.19 | convolution fusion | flops 17201889280 | bytes 35655680 | tf_op jit(solution)/shard_map/kr,cirj->cikj/dot_general | solution.py:88
  393.7 13.0 %gather_fusion = bf16[16,2,1024,256]{2,3,1,0:T(8,128)(2,1)} fusion(bf16[2,16,1024,256]{2,3,1,0:T(8,128)(2,1)} %fusion.10, s32[1024]{0:T(1024)S(1)} %pad_clamp_fusion), kind=kCustom, calls=%fused_computation | custom fusion | bytes 33554496 | tf_op jit(solution)/shard_map/jit(_take)/gather | solution.py:94
  406.8 14.2 %select_bitcast_fusion = bf16[2,16,1024,256]{2,3,0,1:T(8,128)(2,1)} fusion(bf16[16,2,1024,256]{2,3,1,0:T(8,128)(2,1)} %gather_fusion, pred[16]{0:T(512)(128)(4,1)S(1)} %compare_and_fusion), kind=kLoop, calls=%fused_computation.18 | loop fusion | flops 8388608 | bytes 33554448 | tf_op jit(solution)/shard_map/jit(_take)/select_n | solution.py:94
  421.0 41.2 %copy.20 = bf16[2,16,1024,256]{3,0,1,2:T(2,128)(2,1)} copy(bf16[2,16,1024,256]{2,3,0,1:T(8,128)(2,1)} %select_bitcast_fusion) | data formatting | bytes 33554432 | tf_op jit(solution)/shard_map/jit(_take)/select_n | solution.py:94
  462.2 189.1 %all_to_all.41 = bf16[2,16,1024,256]{3,0,1,2:T(2,128)(2,1)S(1)} all-to-all(bf16[2,16,1024,256]{3,0,1,2:T(2,128)(2,1)} %copy.20), channel_id=1, replica_groups=mesh['rad'=4,'mode'=8] {'rad'}, dimensions={2} | all-to-all | bytes 33554432 | tf_op jit(solution)/shard_map/all_to_all | solution.py:96
  651.3 18.9 %copy.21 = bf16[2,16,256,4,256]{4,3,2,0,1:T(4,128)(2,1)} copy(bf16[2,16,256,4,256]{4,0,1,2,3:T(2,128)(2,1)S(1)} %bitcast.53) | data formatting | bytes 33554432 | tf_op jit(solution)/shard_map/all_to_all | solution.py:96
  670.2 27.3 %all_to_all.36 = bf16[2,16,256,1024]{3,2,0,1:T(8,128)(2,1)} reshape(bf16[2,16,256,4,256]{4,3,2,0,1:T(4,128)(2,1)} %copy.21) | data formatting | bytes 33554432 | tf_op jit(solution)/shard_map/all_to_all | solution.py:96
  697.6 365.7 %all_to_all.42 = bf16[2,16,256,1024]{3,2,0,1:T(8,128)(2,1)S(1)} all-to-all(bf16[2,16,256,1024]{3,2,0,1:T(8,128)(2,1)} %all_to_all.36), channel_id=1, replica_groups=mesh['rad'=4,'mode'=8] {'mode'}, dimensions={1} | all-to-all | bytes 33554432 | tf_op jit(solution)/shard_map/all_to_all | solution.py:95
  1063.3 6.7 copy.22
  (6 shorter events, 0.0 us)
Async XLA Ops:
  1.4 15.7 %collective-permute-start = (bf16[2,16,2,1024]{3,2,1,0:T(2,128)(2,1)S(1)}, bf16[2,16,2,1024]{3,2,1,0:T(2,128)(2,1)S(1)}, u32[]{:S(2)}, u32[]{:S(2)}) collective-permute-start(bf16[2,16,2,1024]{3,2,1,0:T(2,128)(2,1)S(1)} %get-tuple-element.5), channel_id=1, source_target_pairs={{0,8},{8,16},{16,24},{1,9},{9,17},{17,25},{2,10},{10,18},{18,26},{... | collective-permute-start | bytes 393224 | tf_op jit(solution)/shard_map/ppermute | solution.py:14
  5.1 12.0 %collective-permute-start.1 = (bf16[2,16,2,1024]{3,2,1,0:T(2,128)(2,1)S(1)}, bf16[2,16,2,1024]{3,2,1,0:T(2,128)(2,1)S(1)}, u32[]{:S(2)}, u32[]{:S(2)}) collective-permute-start(bf16[2,16,2,1024]{3,2,1,0:T(2,128)(2,1)S(1)} %get-tuple-element.6), channel_id=1, source_target_pairs={{8,0},{16,8},{24,16},{9,1},{17,9},{25,17},{10,2},{18,10},{26,18},{... | collective-permute-start | bytes 393224 | tf_op jit(solution)/shard_map/ppermute | solution.py:15
  125.6 7.3 copy-start.1
  125.6 7.9 copy-start
  125.6 186.7 %all-to-all-start = ((bf16[2,16,256,1024]{2,1,0,3:T(8,128)(2,1)}), bf16[2,16,256,1024]{2,1,0,3:T(8,128)(2,1)}, u32[]{:S(2)}, u32[]{:S(2)}) async-start(bf16[2,16,256,1024]{2,1,0,3:T(8,128)(2,1)} %copy.16), calls=%async_computation | async-start | bytes 33554432 | tf_op jit(solution)/shard_map/all_to_all | solution.py:79
  312.3 26.3 %copy-start.2 = (bf16[1024,1024]{1,0:T(8,128)(2,1)S(1)}, bf16[1024,1024]{1,0:T(8,128)(2,1)}, u32[]{:S(2)}) copy-start(bf16[1024,1024]{1,0:T(8,128)(2,1)} %param.11) | copy-start | bytes 6291460
where the time goes:
time: 1080 us; the launch traced here: 1070 us
  blocking collectives  555 us (51%)
  waiting for transfers between devices  172 us (16%)
  local copies, waits for them, and re-layouts  160 us (15%)
  other arithmetic  115 us (11%)
  matrix products  55.1 us (5%)
  starting transfers between devices  12.9 us (1%)
    all_to_all x1, blocking collectives, on_device(): lax.all_to_all(lax.all_to_all(sendable, 'rad', split_axis=2, concat_axis=...  366 us
    all_to_all x1, blocking collectives, on_device(): lax.all_to_all(sendable, 'rad', split_axis=2, concat_axis=3, tiled=True)  189 us
    all_to_all x1, waiting for transfers between devices, on_device(): lax.all_to_all(updated, 'rad', split_axis=3, concat_axis=2, tiled=True)  172 us
    convert_element_type x1, other arithmetic, explicit(): jnp.where(live_mask[None, :, None, :], updated, 0.0).astype(jnp.bfloat16)  65.6 us
    all_to_all x2, local copies, waits for them, and re-layouts, on_device(): lax.all_to_all(sendable, 'rad', split_axis=2, concat_axis=3, tiled=True)  46.2 us
    select_n x1, local copies, waits for them, and re-layouts, on_device(): sendable = jnp.take(solved, picked_rows, axis=1)  41.2 us
    dot_general x1, matrix products, on_device(): jnp.einsum('kr,cirj->cikj', dual_full, relaid, preferred_element_type=jnp...  27.6 us
    dot_general x1, matrix products, on_device(): jnp.einsum('kr,cirj->cikj', basis_full, scaled, preferred_element_type=jn...  27.5 us
  transfers between devices with their start and end apart: 3, of which 1 were waited for; matrix products, arithmetic and copies ran while one was open for 2% of the time, Pallas kernels for 0%

commit v1 on v0

v1 whole, which is shorter than its diff:
```python
import functools

import jax
import jax.numpy as jnp
from jax import lax
from jax.experimental import pallas as pl
from jax.experimental.pallas import tpu as pltpu
from jax.sharding import PartitionSpec as P

SPLIT = 2
AHEAD = 2
SEND_SLOTS = 3
OUT_SLOTS = 4
PAD = 16
TILE = 256
ROWS = 128


def kernel(
    sizes,
    order_ref,
    count_ref,
    spectra_ref,
    kappa_ref,
    eigen_ref,
    basis_ref,
    dual_ref,
    out_ref,
    spec,
    basis,
    dual,
    recv,
    send,
    upd,
    obuf,
    load_sem,
    send_sem,
    recv_sem,
    osend_sem,
    orecv_sem,
):
    parts, modes, rows, shells, slots, orders = sizes
    block = shells // parts
    per = rows // modes
    width = slots // SPLIT
    pairs = 2 * rows // parts
    steps = pairs * SPLIT
    q = lax.axis_index("rad")
    s = lax.axis_index("mode")

    load = pltpu.make_async_copy(spectra_ref, spec, load_sem.at[0])
    load.start()
    load_basis = pltpu.make_async_copy(basis_ref, basis, load_sem.at[1])
    load_basis.start()
    load_dual = pltpu.make_async_copy(dual_ref, dual, load_sem.at[2])
    load_dual.start()

    barrier = pltpu.get_barrier_semaphore()
    count = parts * modes
    me = q * modes + s

    def greet(i, _):
        other = lax.rem(me + i, count)
        pl.semaphore_signal(
            barrier,
            inc=1,
            device_id={"rad": other // modes, "mode": lax.rem(other, modes)},
            device_id_type=pl.DeviceIdType.MESH,
        )
        return 0

    lax.fori_loop(1, count, greet, 0)

    def pair(who, step):
        half = lax.rem(who, 2)
        turn = lax.rem(step // SPLIT + (s * pairs) // modes + 2 * who, pairs)
        p = 2 * turn + half
        return who // 2, p // per, lax.rem(p, per), lax.rem(step, SPLIT)

    def shell_copy(who, step):
        slot = lax.rem(step, SEND_SLOTS)
        return pltpu.make_async_remote_copy(
            src_ref=send.at[slot, who],
            dst_ref=recv.at[step, pl.ds(PAD + q * block, block)],
            send_sem=send_sem.at[slot, who],
            recv_sem=recv_sem.at[step, q],
            device_id={"rad": who, "mode": s},
            device_id_type=pl.DeviceIdType.MESH,
        )

    def read_row(who, step):
        c, d, k, piece = pair(who, step)
        row = lax.rem(order_ref[d * rows + s * per + k], rows)
        cols = pl.ds(pl.multiple_of(piece * width, width), width)
        return spec[c, row, :, cols]

    def push(step):
        slot = lax.rem(step, SEND_SLOTS)

        def one(i, _):
            who = lax.rem(q + i, parts)

            @pl.when(step >= SEND_SLOTS)
            def _():
                shell_copy(who, step - SEND_SLOTS).wait_send()

            send[slot, who] = read_row(who, step)
            shell_copy(who, step).start()
            return 0

        lax.fori_loop(1, parts, one, 0)
        recv[step, pl.ds(PAD + q * block, block), :] = read_row(q, step)

    def arrive(step):
        def one(i, _):
            who = lax.rem(q + i, parts)
            pltpu.make_async_remote_copy(
                src_ref=send.at[0, who],
                dst_ref=recv.at[step, pl.ds(PAD + who * block, block)],
                send_sem=send_sem.at[0, who],
                recv_sem=recv_sem.at[step, who],
                device_id={"rad": who, "mode": s},
                device_id_type=pl.DeviceIdType.MESH,
            ).wait_recv()
            return 0

        lax.fori_loop(1, parts, one, 0)

    def result_copies(step, act_remote, act_local):
        c, d, k, piece = pair(q, step)
        slot = lax.rem(step, OUT_SLOTS)
        cols = pl.ds(pl.multiple_of(piece * width, width), width)

        def one(i, _):
            who = lax.rem(q + i, parts)
            src = obuf.at[slot, pl.ds(who * block, block)]
            dst = out_ref.at[c, s * per + k, :, cols]
            here = (d == s) & (who == q)

            @pl.when(here)
            def _():
                act_local(pltpu.make_async_copy(src, dst, osend_sem.at[slot, who]))

            @pl.when(jnp.logical_not(here))
            def _():
                act_remote(
                    pltpu.make_async_remote_copy(
                        src_ref=src,
                        dst_ref=dst,
                        send_sem=osend_sem.at[slot, who],
                        recv_sem=orecv_sem.at[c, s * per + k],
                        device_id={"rad": who, "mode": d},
                        device_id_type=pl.DeviceIdType.MESH,
                    )
                )

            return 0

        lax.fori_loop(0, parts, one, 0)

    zero_pad = jnp.zeros((PAD, width), jnp.bfloat16)

    def clear(step, _):
        recv[step, pl.ds(0, PAD), :] = zero_pad
        recv[step, pl.ds(PAD + shells, PAD), :] = zero_pad
        return 0

    lax.fori_loop(0, steps, clear, 0)
    load.wait()
    pl.semaphore_wait(barrier, count - 1)
    for first in range(AHEAD):
        push(jnp.int32(first))

    load_basis.wait()
    load_dual.wait()

    def add_identity(i, _):
        at = pl.ds(pl.multiple_of(i * ROWS, ROWS), ROWS)
        row = lax.broadcasted_iota(jnp.int32, (ROWS, shells), 0) + i * ROWS
        col = lax.broadcasted_iota(jnp.int32, (ROWS, shells), 1)
        eye = jnp.where(row == col, 1.0, 0.0).astype(jnp.float32)
        basis[at, :] = (eye + basis[at, :].astype(jnp.float32)).astype(jnp.bfloat16)
        dual[at, :] = (eye + dual[at, :].astype(jnp.float32)).astype(jnp.bfloat16)
        return 0

    lax.fori_loop(0, shells // ROWS, add_identity, 0)

    def body(step, _):
        @pl.when(step + AHEAD < steps)
        def _():
            push(step + AHEAD)

        arrive(step)
        c, d, k, piece = pair(q, step)
        row_id = order_ref[d * rows + s * per + k]
        limit = count_ref[row_id]
        order = (row_id * slots) // (2 * orders)
        slot = lax.rem(step, OUT_SLOTS)

        def table(ct):
            ids = (
                lax.broadcasted_iota(jnp.int32, (1, TILE), 1) + piece * width + ct * TILE
            )
            degree = (order + ids).astype(jnp.float32)
            return degree * (degree + 1.0), ids < limit

        def stencil(i, _):
            ct = lax.rem(i, width // TILE)
            rb = i // (width // TILE)
            at = pl.multiple_of(rb * ROWS, ROWS)
            cols = pl.ds(pl.multiple_of(ct * TILE, TILE), TILE)
            ext = recv[step, pl.ds(at, ROWS + 2 * PAD), cols].astype(jnp.float32)
            size = ROWS + 2 * PAD

            def near(o):
                return pltpu.roll(ext, (size - o) % size, 0)[PAD : PAD + ROWS]

            f = ext[PAD : PAD + ROWS]
            second = (
                16.0 * (near(-1) + near(1)) - (near(-2) + near(2)) - 30.0 * f
            ) * (1.0 / 12.0)
            ll, live = table(ct)
            shell = lax.broadcasted_iota(jnp.int32, (ROWS, 1), 0) + at
            rho = 1.2 + shell.astype(jnp.float32) / shells
            inverse = 1.0 / ((shells * rho) * (shells * rho))
            half = 0.5 * kappa_ref[pl.ds(at, ROWS), :]
            value = f + half * (second - (ll * inverse) * f)
            value = jnp.where(live, value, 0.0)
            upd[pl.ds(at, ROWS), cols] = value.astype(jnp.bfloat16)
            return 0

        lax.fori_loop(0, (shells // ROWS) * (width // TILE), stencil, 0)

        @pl.when(step >= OUT_SLOTS)
        def _():
            result_copies(
                step - OUT_SLOTS, lambda r: r.wait_send(), lambda l: l.wait()
            )

        def transform(ct, _):
            cols = pl.ds(pl.multiple_of(ct * TILE, TILE), TILE)
            ll, live = table(ct)
            projected = jnp.dot(
                dual[...], upd[:, cols], preferred_element_type=jnp.float32
            )
            divisor = eigen_ref[...] + ll * (0.5 / (slots * slots))
            scaled = (projected / divisor).astype(jnp.bfloat16)
            restored = jnp.dot(basis[...], scaled, preferred_element_type=jnp.float32)
            obuf[slot, :, cols] = jnp.where(live, restored, 0.0).astype(jnp.bfloat16)
            return 0

        lax.fori_loop(0, width // TILE, transform, 0)
        result_copies(step, lambda r: r.start(), lambda l: l.start())
        return 0

    lax.fori_loop(0, steps, body, 0)

    def drain_send(i, _):
        step = steps - SEND_SLOTS + i // (parts - 1)
        who = lax.rem(q + 1 + lax.rem(i, parts - 1), parts)
        shell_copy(who, step).wait_send()
        return 0

    lax.fori_loop(0, SEND_SLOTS * (parts - 1), drain_send, 0)

    def drain_out(i, _):
        result_copies(
            steps - OUT_SLOTS + i, lambda r: r.wait_send(), lambda l: l.wait()
        )
        return 0

    lax.fori_loop(0, OUT_SLOTS, drain_out, 0)

    def landed(i, _):
        c = i // rows
        row = lax.rem(i, rows)
        source = row // per
        p = s * per + lax.rem(row, per)
        who = 2 * c + lax.rem(p, 2)

        @pl.when(jnp.logical_not((source == s) & (who == q)))
        def _():
            pltpu.make_async_remote_copy(
                src_ref=out_ref.at[c, row],
                dst_ref=out_ref.at[c, row],
                send_sem=osend_sem.at[0, 0],
                recv_sem=orecv_sem.at[c, row],
                device_id={"rad": who, "mode": source},
                device_id_type=pl.DeviceIdType.MESH,
            ).wait_recv()

        return 0

    lax.fori_loop(0, 2 * rows, landed, 0)


def on_device(
    spectra, diffusivity, eigenvalues, radial_basis, dual_basis, degree_count, order_slot
):
    _, rows, block, slots = spectra.shape
    shells = diffusivity.shape[0]
    orders = degree_count.shape[0]
    parts = lax.axis_size("rad")
    modes = lax.axis_size("mode")
    steps = 2 * rows // parts * SPLIT
    width = slots // SPLIT
    bf16 = jnp.bfloat16
    dma = pltpu.SemaphoreType.DMA
    sizes = (parts, modes, rows, shells, slots, orders)
    vmem = pl.BlockSpec(memory_space=pltpu.VMEM)
    smem = pl.BlockSpec(memory_space=pltpu.SMEM)
    hbm = pl.BlockSpec(memory_space=pl.ANY)
    return pl.pallas_call(
        functools.partial(kernel, sizes),
        out_shape=jax.ShapeDtypeStruct(spectra.shape, bf16),
        in_specs=[smem, smem, hbm, vmem, vmem, hbm, hbm],
        out_specs=hbm,
        scratch_shapes=[
            pltpu.VMEM(spectra.shape, bf16),
            pltpu.VMEM((shells, shells), bf16),
            pltpu.VMEM((shells, shells), bf16),
            pltpu.VMEM((steps, shells + 2 * PAD, width), bf16),
            pltpu.VMEM((SEND_SLOTS, parts, block, width), bf16),
            pltpu.VMEM((shells, width), bf16),
            pltpu.VMEM((OUT_SLOTS, shells, width), bf16),
            dma((3,)),
            dma((SEND_SLOTS, parts)),
            dma((steps, parts)),
            dma((OUT_SLOTS, parts)),
            dma((2, rows)),
        ],
        compiler_params=pltpu.CompilerParams(
            collective_id=0,
            has_side_effects=True,
            vmem_limit_bytes=60 * 1024 * 1024,
        ),
    )(
        order_slot,
        degree_count,
        spectra,
        diffusivity.reshape(shells, 1),
        eigenvalues.reshape(shells, 1),
        radial_basis,
        dual_basis,
    )


def solution(mesh):
    placed = (P(None, "mode", "rad", None), P(), P(), P(), P(), P(), P())
    return jax.shard_map(
        on_device,
        mesh=mesh,
        in_specs=placed,
        out_specs=P(None, "mode", "rad", None),
        check_vma=False,
    )
```

time: 1080 us -> 476 us (0.44)
  blocking collectives: 555 us -> 0 us
  Pallas kernels: 0 us -> 457 us
  waiting for transfers between devices: 172 us -> 0 us
  local copies, waits for them, and re-layouts: 160 us -> 17.3 us
  other arithmetic: 115 us -> 0 us
  matrix products: 55.1 us -> 0 us
  starting transfers between devices: 12.9 us -> 0 us
    all_to_all x2 -> x0, blocking collectives: 555 us -> none  [the longest x1 366 us: on_device(): lax.all_to_all(lax.all_to_all(sendable, 'rad', split_axis=2, concat_axis=...]
    pallas_call x0 -> x1, Pallas kernels: none -> 457 us  [on_device(): pl.pallas_call(functools.partial(kernel, sizes), out_shape=jax.ShapeDtype...]
    all_to_all x1 -> x0, waiting for transfers between devices: 172 us -> none  [on_device(): lax.all_to_all(updated, 'rad', split_axis=3, concat_axis=2, tiled=True)]
    convert_element_type x2 -> x0, other arithmetic: 84.8 us -> none  [the longest x1 65.6 us: explicit(): jnp.where(live_mask[None, :, None, :], updated, 0.0).astype(jnp.bfloat16)]
    all_to_all x4 -> x0, local copies, waits for them, and re-layouts: 79.3 us -> none  [the longest x2 46.2 us: on_device(): lax.all_to_all(sendable, 'rad', split_axis=2, concat_axis=3, tiled=True)]
    dot_general x2 -> x0, matrix products: 55.1 us -> none  [the longest x1 27.6 us: on_device(): jnp.einsum('kr,cirj->cikj', dual_full, relaid, preferred_element_type=jnp...]
    select_n x1 -> x0, local copies, waits for them, and re-layouts: 41.2 us -> none  [on_device(): sendable = jnp.take(solved, picked_rows, axis=1)]
    convert_element_type x1 -> x0, local copies, waits for them, and re-layouts: 23.7 us -> none  [explicit(): jnp.where(live_mask[None, :, None, :], updated, 0.0).astype(jnp.bfloat16)]
  transfers between devices with their start and end apart: 3 -> 0, of which waited for: 1 -> 0; matrix products, arithmetic and copies ran while one was open for 2% -> 0% of each run, Pallas kernels for 0% -> 0%
where the time goes in v1:
time: 476 us; the launch traced here: 475 us
  Pallas kernels  457 us (96%)
  local copies, waits for them, and re-layouts  17.3 us (4%)
    pallas_call x1, Pallas kernels, on_device(): pl.pallas_call(functools.partial(kernel, sizes), out_shape=jax.ShapeDtype...  457 us
    unnamed x1, local copies, waits for them, and re-layouts  13.9 us

profile of v1, /device:TPU:25, one launch (start us, length us, event | category | flops | bytes accessed | tf_op | source)
XLA Modules:
  0.0 474.8 jit_solution(1103228333150137221)
XLA Ops:
  0.0 1.7 copy.8.kappa_ref
  1.7 1.7 copy.9.eigen_ref
  3.4 457.5 %shard_map.73 = bf16[2,16,256,1024]{3,2,1,0:T(8,128)(2,1)} custom-call(s32[128]{0:T(128)} %order_ref.1, s32[128]{0:T(128)} %count_ref.1, bf16[2,16,256,1024]{3,2,1,0:T(8,128)(2,1)} %spectra_ref.1, f32[1024,1]{1,0:T(8,128)} %copy.8.kappa_ref, f32[1024,1]{1,0:T(8,128)} %copy.9.eigen_ref, bf16[1024,1024]{1,0:T(8,128)(2,1)} %basis_ref.1, bf16[1024,1024]{1,0:T(8,128)(2,1)} %dual_ref.1), custom_call_target="tpu_custom_call" | custom-call | tf_op jit(solution)/shard_map/pallas_call | solution.py:313
  460.9 13.9 %copy.11 = bf16[2,16,256,1024]{3,2,1,0:T(8,128)(2,1)} copy(bf16[2,16,256,1024]{3,2,1,0:T(8,128)(2,1)} %shard_map.73) | data formatting | bytes 33554432

commit v2 on v1

--- a/solution.py
+++ b/solution.py
@@ -7,6 +7,7 @@
 from jax.experimental.pallas import tpu as pltpu
 from jax.sharding import PartitionSpec as P
 
+LANES = 128
 SPLIT = 2
 AHEAD = 2
 SEND_SLOTS = 3
@@ -33,11 +34,13 @@
     send,
     upd,
     obuf,
+    zeros,
     load_sem,
     send_sem,
     recv_sem,
     osend_sem,
     orecv_sem,
+    fill_sem,
 ):
     parts, modes, rows, shells, slots, orders = sizes
     block = shells // parts
@@ -48,6 +51,23 @@
     q = lax.axis_index("rad")
     s = lax.axis_index("mode")
 
+    def live_width(group):
+        most = slots - (group * rows * slots) // (2 * orders)
+        return (most + LANES - 1) // LANES * LANES
+
+    least = slots - ((modes - 1) * rows * slots) // (2 * orders)
+    least = (least + LANES - 1) // LANES * LANES
+    wholes = range(least, slots + 1, LANES)
+    widths = sorted({min(max(w - i * width, 0), width) for w in wholes for i in range(SPLIT)})
+
+    def sized(value, choices, act):
+        for choice in choices:
+            if choice:
+                pl.when(value == choice)(functools.partial(act, choice))
+
+    def piece_width(group, piece):
+        return jnp.clip(live_width(group) - piece * width, 0, width)
+
     load = pltpu.make_async_copy(spectra_ref, spec, load_sem.at[0])
     load.start()
     load_basis = pltpu.make_async_copy(basis_ref, basis, load_sem.at[1])
@@ -77,11 +97,18 @@
         p = 2 * turn + half
         return who // 2, p // per, lax.rem(p, per), lax.rem(step, SPLIT)
 
-    def shell_copy(who, step):
+    def shell_copy(who, step, act):
+        sized(
+            piece_width(s, lax.rem(step, SPLIT)),
+            widths,
+            lambda w: act(shell_copy_of(who, step, w)),
+        )
+
+    def shell_copy_of(who, step, w):
         slot = lax.rem(step, SEND_SLOTS)
         return pltpu.make_async_remote_copy(
-            src_ref=send.at[slot, who],
-            dst_ref=recv.at[step, pl.ds(PAD + q * block, block)],
+            src_ref=send.at[slot, who, :, pl.ds(0, w)],
+            dst_ref=recv.at[step, pl.ds(PAD + q * block, block), pl.ds(0, w)],
             send_sem=send_sem.at[slot, who],
             recv_sem=recv_sem.at[step, q],
             device_id={"rad": who, "mode": s},
@@ -102,26 +129,40 @@
 
             @pl.when(step >= SEND_SLOTS)
             def _():
-                shell_copy(who, step - SEND_SLOTS).wait_send()
+                shell_copy(who, step - SEND_SLOTS, lambda r: r.wait_send())
 
             send[slot, who] = read_row(who, step)
-            shell_copy(who, step).start()
+            shell_copy(who, step, lambda r: r.start())
             return 0
 
         lax.fori_loop(1, parts, one, 0)
-        recv[step, pl.ds(PAD + q * block, block), :] = read_row(q, step)
+
+        def keep(w):
+            c, d, k, piece = pair(q, step)
+            row = lax.rem(order_ref[d * rows + s * per + k], rows)
+            cols = pl.ds(pl.multiple_of(piece * width, width), w)
+            recv[step, pl.ds(PAD + q * block, block), pl.ds(0, w)] = spec[c, row, :, cols]
+
+        sized(piece_width(s, lax.rem(step, SPLIT)), widths, keep)
 
     def arrive(step):
         def one(i, _):
             who = lax.rem(q + i, parts)
-            pltpu.make_async_remote_copy(
-                src_ref=send.at[0, who],
-                dst_ref=recv.at[step, pl.ds(PAD + who * block, block)],
-                send_sem=send_sem.at[0, who],
-                recv_sem=recv_sem.at[step, who],
-                device_id={"rad": who, "mode": s},
-                device_id_type=pl.DeviceIdType.MESH,
-            ).wait_recv()
+
+
+            def wait(w):
+                pltpu.make_async_remote_copy(
+                    src_ref=send.at[0, who, :, pl.ds(0, w)],
+                    dst_ref=recv.at[
+                        step, pl.ds(PAD + who * block, block), pl.ds(0, w)
+                    ],
+                    send_sem=send_sem.at[0, who],
+                    recv_sem=recv_sem.at[step, who],
+                    device_id={"rad": who, "mode": s},
+                    device_id_type=pl.DeviceIdType.MESH,
+                ).wait_recv()
+
+            sized(piece_width(s, lax.rem(step, SPLIT)), widths, wait)
             return 0
 
         lax.fori_loop(1, parts, one, 0)
@@ -129,11 +170,15 @@
     def result_copies(step, act_remote, act_local):
         c, d, k, piece = pair(q, step)
         slot = lax.rem(step, OUT_SLOTS)
-        cols = pl.ds(pl.multiple_of(piece * width, width), width)
 
         def one(i, _):
             who = lax.rem(q + i, parts)
-            src = obuf.at[slot, pl.ds(who * block, block)]
+            sized(piece_width(s, piece), widths, functools.partial(send_block, who))
+            return 0
+
+        def send_block(who, w):
+            cols = pl.ds(pl.multiple_of(piece * width, width), w)
+            src = obuf.at[slot, pl.ds(who * block, block), pl.ds(0, w)]
             dst = out_ref.at[c, s * per + k, :, cols]
             here = (d == s) & (who == q)
 
@@ -154,8 +199,6 @@
                     )
                 )
 
-            return 0
-
         lax.fori_loop(0, parts, one, 0)
 
     zero_pad = jnp.zeros((PAD, width), jnp.bfloat16)
@@ -163,8 +206,35 @@
     def clear(step, _):
         recv[step, pl.ds(0, PAD), :] = zero_pad
         recv[step, pl.ds(PAD + shells, PAD), :] = zero_pad
-        return 0
-
+
+        def clear_dead(w):
+            if w < width:
+                recv[step, pl.ds(PAD, shells), pl.ds(w, width - w)] = jnp.zeros(
+                    (shells, width - w), jnp.bfloat16
+                )
+
+        sized(piece_width(s, lax.rem(step, SPLIT)), widths, clear_dead)
+        return 0
+
+    def fill(i, act):
+        c = i // rows
+        row = lax.rem(i, rows)
+
+        def one(w):
+            if w < slots:
+                act(
+                    pltpu.make_async_copy(
+                        zeros.at[:, pl.ds(0, slots - w)],
+                        out_ref.at[c, row, :, pl.ds(w, slots - w)],
+                        fill_sem.at[c, row],
+                    )
+                )
+
+        sized(live_width(row // per), wholes, one)
+        return 0
+
+    zeros[...] = jnp.zeros_like(zeros)
+    lax.fori_loop(0, 2 * rows, lambda i, _: fill(i, lambda r: r.start()), 0)
     lax.fori_loop(0, steps, clear, 0)
     load.wait()
     pl.semaphore_wait(barrier, count - 1)
@@ -258,7 +328,7 @@
     def drain_send(i, _):
         step = steps - SEND_SLOTS + i // (parts - 1)
         who = lax.rem(q + 1 + lax.rem(i, parts - 1), parts)
-        shell_copy(who, step).wait_send()
+        shell_copy(who, step, lambda r: r.wait_send())
         return 0
 
     lax.fori_loop(0, SEND_SLOTS * (parts - 1), drain_send, 0)
@@ -278,19 +348,23 @@
         p = s * per + lax.rem(row, per)
         who = 2 * c + lax.rem(p, 2)
 
-        @pl.when(jnp.logical_not((source == s) & (who == q)))
-        def _():
+        def wait(w):
             pltpu.make_async_remote_copy(
-                src_ref=out_ref.at[c, row],
-                dst_ref=out_ref.at[c, row],
+                src_ref=out_ref.at[c, row, :, pl.ds(0, w)],
+                dst_ref=out_ref.at[c, row, :, pl.ds(0, w)],
                 send_sem=osend_sem.at[0, 0],
                 recv_sem=orecv_sem.at[c, row],
                 device_id={"rad": who, "mode": source},
                 device_id_type=pl.DeviceIdType.MESH,
             ).wait_recv()
 
-        return 0
-
+        @pl.when(jnp.logical_not((source == s) & (who == q)))
+        def _():
+            sized(live_width(source), wholes, wait)
+
+        return 0
+
+    lax.fori_loop(0, 2 * rows, lambda i, _: fill(i, lambda r: r.wait()), 0)
     lax.fori_loop(0, 2 * rows, landed, 0)
 
 
@@ -323,10 +397,12 @@
             pltpu.VMEM((SEND_SLOTS, parts, block, width), bf16),
             pltpu.VMEM((shells, width), bf16),
             pltpu.VMEM((OUT_SLOTS, shells, width), bf16),
+            pltpu.VMEM((block, slots // 2), bf16),
             dma((3,)),
             dma((SEND_SLOTS, parts)),
             dma((steps, parts)),
             dma((OUT_SLOTS, parts)),
+            dma((2, rows)),
             dma((2, rows)),
         ],
         compiler_params=pltpu.CompilerParams(

time: 476 us -> 450 us (0.945)
  Pallas kernels: 457 us -> 432 us
    pallas_call x1, Pallas kernels: 457 us -> 432 us  [on_device(): pl.pallas_call(functools.partial(kernel, sizes), out_shape=jax.ShapeDtype...]
where the time goes in v2:
time: 450 us
  Pallas kernels  432 us (96%)
  local copies, waits for them, and re-layouts  17.3 us (4%)
    pallas_call x1, Pallas kernels, on_device(): pl.pallas_call(functools.partial(kernel, sizes), out_shape=jax.ShapeDtype...  432 us
    unnamed x1, local copies, waits for them, and re-layouts  13.9 us

profile of v2, /device:TPU:25, one launch (start us, length us, event | category | flops | bytes accessed | tf_op | source)
XLA Modules:
  0.0 449.6 jit_solution(8925699284060363402)
XLA Ops:
  0.0 1.7 copy.8.kappa_ref
  1.7 1.7 copy.9.eigen_ref
  3.4 432.3 %shard_map.73 = bf16[2,16,256,1024]{3,2,1,0:T(8,128)(2,1)} custom-call(s32[128]{0:T(128)} %order_ref.1, s32[128]{0:T(128)} %count_ref.1, bf16[2,16,256,1024]{3,2,1,0:T(8,128)(2,1)} %spectra_ref.1, f32[1024,1]{1,0:T(8,128)} %copy.8.kappa_ref, f32[1024,1]{1,0:T(8,128)} %copy.9.eigen_ref, bf16[1024,1024]{1,0:T(8,128)(2,1)} %basis_ref.1, bf16[1024,1024]{1,0:T(8,128)(2,1)} %dual_ref.1), custom_call_target="tpu_custom_call" | custom-call | tf_op jit(solution)/shard_map/pallas_call | solution.py:387
  435.7 13.9 %copy.11 = bf16[2,16,256,1024]{3,2,1,0:T(8,128)(2,1)} copy(bf16[2,16,256,1024]{3,2,1,0:T(8,128)(2,1)} %shard_map.73) | data formatting | bytes 33554432
